TPU v7x, 256 devices: a whole 4x4x8 slice. The times are simulated.
256 devices in a mesh: rep: 32 (over z, x_hi, core), fsdp: 8 (over x_lo, y).
Axes of the slice: x: 4 (x_hi: 2, x_lo: 2; x = x_hi * 2 + x_lo), y: 4, z: 8, core: 2. Of those that a mesh axis runs over, the one named last changes fastest.
Arguments:
- tokens: bfloat16 [65536, 5120], P(('rep', 'fsdp')), may hold values from -6 to 6
- cotangent: bfloat16 [65536, 5120], P(('rep', 'fsdp')), may hold values from -0.119628906 to 0.119628906
- token_row: int32 [65536], P(('rep', 'fsdp')), may hold values from 0 to 43
- token_col: int32 [65536], P(('rep', 'fsdp')), may hold values from 0 to 79
- token_frame: int32 [65536], P(('rep', 'fsdp')), may hold values from 0 to 23
- token_camera: int32 [65536], P(('rep', 'fsdp')), may hold values from 0 to 3
- pixel_depth: float32 [128, 65536], P(None, ('rep', 'fsdp')), may hold values from 0.5 to 4
- cam_poses: float32 [32, 12, 96], P('rep'), may hold values from -3 to 3, as said below
- cam_weight: bfloat16 [32, 768, 5120], P('rep', 'fsdp'), may hold values from -0.21875 to 0.21875
- gain: float32 [32, 5120], P('rep'), may hold values from 0.1 to 1.9
- frag_stack: bfloat16 [32, 6, 5120, 256], P('rep', None, 'fsdp'), may hold values from -6 to 6
- frag_block: int32 [6], replicated, may hold values from 0 to 5, each once
- global_frag: float32 [5120, 256], P('fsdp'), may hold values from -6 to 6
- momentum: float32 [5120, 256], P('fsdp'), may hold values from -3 to 3
Outputs:
- cam_grad: bfloat16 [32, 768, 5120], P('rep', 'fsdp')
- gain_grad: float32 [32, 5120], P('rep', 'fsdp')
- new_global: float32 [5120, 256], P('fsdp')
- new_momentum: float32 [5120, 256], P('fsdp')
- merged_frag: bfloat16 [32, 5120, 256], P('rep', 'fsdp')
Inputs may be any that keep to these rules, and one draw needn't show every extreme that they name: `frag_block`: each held block appears once; entry 0 is the block that syncs now. `cam_poses`: for every pose, entries 0 to 8 form a rotation matrix in row-major order; entries 9 to 11 are the camera position.
All inputs are finite; a program needn't handle non-finite values.
Results may differ from a plain program's by a relative error of at most 0.014.
Values may be sent and summed in bfloat16 or wider, within the bound.
A program may use at most 128 MiB of HBM per device.

v0:
```python
import jax
import jax.numpy as jnp
from jax import lax
from jax.sharding import PartitionSpec as P

PIX = 128
NFRAME = 24
GH = 44
GW = 80


EPS = 1e-06
MOMENTUM_RATE = 0.9
OUTER_RATE = 0.7
MIX_RATE = 0.5


def ray_features(token_row, token_col, token_frame, token_camera, pixel_depth, poses):
    count_tok = token_row.shape[0]
    pose_index = token_camera * NFRAME + token_frame
    table = lax.broadcasted_iota(jnp.int32, (poses.shape[1], count_tok), 0)
    one_hot = (table == pose_index[None, :]).astype(jnp.float32)
    per_token = jnp.dot(poses, one_hot, precision=lax.Precision.HIGHEST)
    pixel = lax.broadcasted_iota(jnp.int32, (PIX, 1), 0)
    sub_rows = PIX // 16
    across = (token_col[None, :] * 16 + pixel % 16).astype(jnp.float32)
    down = (token_row[None, :] * sub_rows + pixel // 16).astype(jnp.float32)
    horiz = (across + 0.5) / (GW * 16) * 2.0 - 1.0
    vert = (down + 0.5) / (GH * sub_rows) * 2.0 - 1.0
    dir_x = per_token[0][None, :] * horiz + per_token[1][None, :] * vert + per_token[2][None, :]
    dir_y = per_token[3][None, :] * horiz + per_token[4][None, :] * vert + per_token[5][None, :]
    dir_z = per_token[6][None, :] * horiz + per_token[7][None, :] * vert + per_token[8][None, :]
    length = jnp.sqrt(dir_x * dir_x + dir_y * dir_y + dir_z * dir_z)
    unit_x = dir_x / length
    unit_y = dir_y / length
    unit_z = dir_z / length
    near_x = unit_x / pixel_depth
    near_y = unit_y / pixel_depth
    near_z = unit_z / pixel_depth
    point_x = per_token[9][None, :] + pixel_depth * unit_x
    point_y = per_token[10][None, :] + pixel_depth * unit_y
    point_z = per_token[11][None, :] + pixel_depth * unit_z
    stacked = jnp.stack([near_x, near_y, near_z, point_x, point_y, point_z])
    return stacked.reshape(6 * PIX, count_tok).astype(jnp.bfloat16)


def nesterov(global_part, moment_part, average):
    delta = global_part - average
    moment_next = MOMENTUM_RATE * moment_part + delta
    global_next = global_part - OUTER_RATE * (MOMENTUM_RATE * moment_next + delta)
    return (global_next, moment_next)


def shards(
    tokens,
    cotangent,
    token_row,
    token_col,
    token_frame,
    token_camera,
    pixel_depth,
    cam_poses,
    cam_weight,
    gain,
    frag_stack,
    frag_block,
    global_frag,
    momentum,
):
    rays = ray_features(token_row, token_col, token_frame, token_camera, pixel_depth, cam_poses[0])
    block = rays
    lifted = lax.dot_general(
        block,
        lax.all_gather(cam_weight[0], "fsdp", axis=0, tiled=True),
        (((0,), (0,)), ((), ())),
        preferred_element_type=jnp.float32,
    )
    hidden = tokens.astype(jnp.float32) + lifted
    scale = lax.rsqrt(jnp.mean(hidden * hidden, axis=1, keepdims=True) + EPS)
    normed = hidden * scale
    upstream = cotangent.astype(jnp.float32)
    gain_local = jnp.sum(upstream * normed, axis=0)
    pushed = upstream * gain[0][None, :]
    slope = (scale * (pushed - normed * jnp.mean(pushed * normed, axis=1, keepdims=True))).astype(
        jnp.bfloat16
    )
    gain_grad = lax.psum_scatter(gain_local, "fsdp", scatter_dimension=0, tiled=True)
    block = rays
    weight_grad = lax.psum_scatter(
        jnp.dot(block, slope, preferred_element_type=jnp.float32),
        "fsdp",
        scatter_dimension=0,
        tiled=True,
    )
    chosen = lax.dynamic_index_in_dim(frag_stack[0], frag_block[0], 0, keepdims=False).astype(
        jnp.float32
    )
    replicas = lax.axis_size("rep")
    average = lax.psum(chosen.astype(jnp.bfloat16), "rep").astype(jnp.float32) / replicas
    new_global, new_momentum = nesterov(global_frag, momentum, average)
    merged_frag = (MIX_RATE * chosen + (1.0 - MIX_RATE) * new_global).astype(jnp.bfloat16)
    return (
        weight_grad.astype(jnp.bfloat16)[None],
        gain_grad[None],
        new_global,
        new_momentum,
        merged_frag[None],
    )


def solution(mesh):
    placed = (
        P(("rep", "fsdp"), None),
        P(("rep", "fsdp"), None),
        P(("rep", "fsdp")),
        P(("rep", "fsdp")),
        P(("rep", "fsdp")),
        P(("rep", "fsdp")),
        P(None, ("rep", "fsdp")),
        P("rep", None, None),
        P("rep", "fsdp", None),
        P("rep", None),
        P("rep", None, "fsdp", None),
        P(),
        P("fsdp", None),
        P("fsdp", None),
    )
    return jax.shard_map(
        shards,
        mesh=mesh,
        in_specs=placed,
        out_specs=(
            P("rep", "fsdp", None),
            P("rep", "fsdp"),
            P("fsdp", None),
            P("fsdp", None),
            P("rep", "fsdp", None),
        ),
        check_vma=False,
    )
```

profile of v0, /device:TPU:2, one launch (start us, length us, event | category | flops | bytes accessed | tf_op | source)
XLA Modules:
  0.0 470.5 jit_solution(12593787493489047120)
XLA Ops:
  8.0 0.0 all-gather.3.cloned.1.call-start
  8.0 0.7 all-gather.3.cloned.1.call-update
  8.7 0.0 all-reduce.3.cloned.1.call-start
  10.7 1.7 dynamic-slice_bitcast_fusion
  12.4 0.0 all-reduce.3.cloned.1.call-update
  12.5 0.0 reduce-scatter.2.cloned.1.call-start
  12.5 0.7 multiply_add_fusion.2
  13.2 0.8 convolution_bitcast_fusion
  14.1 0.7 broadcast_multiply_fusion.1
  14.8 1.1 bitcast_dynamic-update-slice_fusion.5
  15.9 1.1 bitcast_dynamic-update-slice_fusion.4
  17.1 1.1 bitcast_dynamic-update-slice_fusion.3
  18.2 1.2 bitcast_dynamic-update-slice_fusion.2
  19.4 1.2 bitcast_dynamic-update-slice_fusion.1
  20.5 1.2 bitcast_dynamic-update-slice_fusion
  21.7 81.5 %all-gather.3.cloned.1.call-done = bf16[1,768,5120]{2,1,0:T(8,128)(2,1)} async-done(((bf16[1,96,5120]{2,1,0:T(8,128)(2,1)}), bf16[1,768,5120]{2,1,0:T(8,128)(2,1)}) %all-gather.3.cloned.1.call-update) | async-done | bytes 7864336 | tf_op jit(solution)/shard_map/all_gather | solution.py:74
  103.2 0.0 copy-start
  103.2 0.0 copy-start.3
  103.2 7.1 %multiply_reduce_fusion = (f32[256]{0:T(256)S(1)}, f32[256,5120]{1,0:T(8,128)S(1)}) fusion(bf16[768,256]{1,0:T(8,128)(2,1)S(1)} %bitcast.51, bf16[1,768,5120]{2,1,0:T(8,128)(2,1)} %all-gather.3.cloned.1.call-done, bf16[256,5120]{1,0:T(8,128)(2,1)} %param.14), kind=kOutput, calls=%fused_computation.11 | convolution fusion | flops 2018508544 | bytes 16122880 | tf_op jit(solution)/shard_map/dot_general | solution.py:72
  110.3 0.0 copy-done
  110.3 0.0 copy-done.3
  110.3 2.0 fusion.10
  112.3 8.1 %fusion.11 = f32[768,5120]{1,0:T(8,128)} fusion(bf16[768,256]{1,0:T(8,128)(2,1)S(1)} %bitcast.52, bf16[256,5120]{1,0:T(8,128)(2,1)S(1)} %copy-done, f32[256,5120]{1,0:T(8,128)S(1)} %get-tuple-element.23, f32[256]{0:T(256)S(1)} %broadcast_multiply_fusion, f32[5120]{0:T(1024)S(1)} %bitcast.54, f32[256]{0:T(256)S(1)} %add_rsqrt_fusion), kind=kOutput, calls=%fused_computation.12 | convolution fusion | flops 2022440960 | bytes 24008704 | tf_op jit(solution)/shard_map/dot_general | solution.py:90
  120.4 0.0 copy-start.4
  120.5 0.0 copy-start.1
  120.5 0.0 copy-start.2
  120.5 0.0 reduce-scatter.2.cloned.1.call-update
  120.5 0.6 copy-done.4
  121.1 0.6 dynamic-slice.1
  122.4 301.8 %all-reduce.3.cloned.1.call-done = bf16[640,256]{1,0:T(8,128)(2,1)} async-done(((bf16[640,256]{1,0:T(8,128)(2,1)}), bf16[640,256]{1,0:T(8,128)(2,1)}) %all-reduce.3.cloned.1.call-update) | async-done | bytes 327696 | tf_op jit(solution)/shard_map/psum | solution.py:99
  424.2 0.0 copy-done.1
  424.2 0.0 copy-done.2
  424.2 2.4 fusion.17
  426.6 33.2 %all-reduce = f32[5120]{0:T(1024)S(1)} all-reduce(f32[5120]{0:T(1024)S(1)} %get-tuple-element.5), channel_id=4, replica_groups=mesh['rep'=32,'fsdp'=8] {'fsdp'}, use_global_device_ids=true, to_apply=%region_4.5.clone | all-reduce | flops 5120 | bytes 40960
  459.8 0.1 dynamic-slice.2
  459.9 0.6 broadcast_in_dim.7
  460.5 0.0 reduce-scatter.2.cloned.1.call-done
  460.5 2.6 convert_bitcast_fusion
  (4 shorter events, 0.0 us)
Async XLA Ops:
  8.0 95.2 %all-gather.3.cloned.1.call-start = ((), (), s32[]{:S(2)}) async-start(), calls=%async_computation.3 | async-start | bytes 8847360 | tf_op jit(solution)/shard_map/all_gather | solution.py:74
  8.7 415.5 %all-reduce.3.cloned.1.call-start = ((), (), s32[]{:S(2)}) async-start(), calls=%async_computation.2 | async-start | bytes 655360 | tf_op jit(solution)/shard_map/psum | solution.py:99
  12.5 448.0 %reduce-scatter.2.cloned.1.call-start = ((), (), s32[]{:S(2)}) async-start(), calls=%async_computation.1 | async-start | bytes 17694720 | tf_op jit(solution)/shard_map/reduce_scatter | solution.py:89
  103.2 7.1 %copy-start = (bf16[256,5120]{1,0:T(8,128)(2,1)S(1)}, bf16[256,5120]{1,0:T(8,128)(2,1)}, u32[]{:S(2)}) copy-start(bf16[256,5120]{1,0:T(8,128)(2,1)} %param.15) | copy-start | bytes 7864324
  103.2 7.1 %copy-start.3 = (f32[1,5120]{1,0:T(1,128)S(1)}, f32[1,5120]{1,0:T(1,128)}, u32[]{:S(2)}) copy-start(f32[1,5120]{1,0:T(1,128)} %param.23) | copy-start | bytes 61444
  120.4 0.7 copy-start.4
  120.5 303.7 %copy-start.1 = (f32[640,256]{1,0:T(8,128)S(1)}, f32[640,256]{1,0:T(8,128)}, u32[]{:S(2)}) copy-start(f32[640,256]{1,0:T(8,128)} %param.26) | copy-start | bytes 1966084
  120.5 303.7 %copy-start.2 = (f32[640,256]{1,0:T(8,128)S(1)}, f32[640,256]{1,0:T(8,128)}, u32[]{:S(2)}) copy-start(f32[640,256]{1,0:T(8,128)} %param.27) | copy-start | bytes 1966084
Sparse Core Ops, SparseCore 0:
  10.6 92.5 all-gather.2
  120.6 164.7 reduce-scatter.1
Sparse Core Ops, SparseCore 1:
  12.6 411.6 all-reduce.2
where the time goes:
time: 471 us
  waiting for transfers between devices  384 us (82%)
  blocking collectives  33.2 us (7%)
  between operations  18.2 us (4%)
  matrix products  16 us (3%)
  other arithmetic  15.4 us (3%)
    psum x1, waiting for transfers between devices, shards(): lax.psum(chosen.astype(jnp.bfloat16), 'rep').astype(jnp.float32) / replicas  302 us
    all_gather x1, waiting for transfers between devices, shards(): lax.all_gather(cam_weight[0], 'fsdp', axis=0, tiled=True)  81.5 us
    unnamed x1, blocking collectives  33.2 us
  transfers between devices with their start and end apart: 3, of which 2 were waited for; matrix products, arithmetic and copies ran while one was open for 7% of the time, Pallas kernels for 0%

commit v1 on v0

v1 whole, which is shorter than its diff:
```python
import jax
import jax.numpy as jnp
from jax import lax
from jax.experimental import pallas as pl
from jax.experimental.pallas import tpu as pltpu
from jax.sharding import PartitionSpec as P

D = 5120
PIX = 128
NFRAME = 24
GH = 44
GW = 80
PIN = 768
POSES = 96
N_REP = 32
SHARE = 8
DS = D // SHARE
ROWS = PIN // SHARE
TOK = 256
CHUNKS = 4
TC = TOK // CHUNKS
CT = SHARE * TC
FR = 640
FP = 80
MSG = TOK + 16

EPS = 1e-06
MOMENTUM_RATE = 0.9
OUTER_RATE = 0.7
MIX_RATE = 0.5

MESH = pl.DeviceIdType.MESH
F32 = jnp.float32
BF16 = jnp.bfloat16


def spread(row):
    return jnp.broadcast_to(row, (128, 128)).T


def kernel(
    tok, cot, trow, tcol, tfr, tcam, depth, poses, weight, gain, frag, block, glob, mom,
    grad_out, gain_out, glob_out, mom_out, merged_out,
    tokv, cotv, wv, msg, depthv, idxv, posev, gainv, table_hi, table_lo,
    rays_t, rays, hid, slope, acc, grad, gacc, stat,
    fragv, chosen, fpart, fsum, fother, avg, globv, momv, mergedv,
    lsem, main_s, main_r, w_s, w_r, msg_s, msg_r, st_s, st_r, g_s, g_r,
    f_s, f_r, h_s, h_r, b_s, b_r,
):
    rep, me = lax.axis_index("rep"), lax.axis_index("fsdp")
    z, xh, core = rep // 4, lax.rem(rep // 2, 2), lax.rem(rep, 2)

    def flip(a, b, bits):
        out = a
        for i in range(bits):
            if b >> i & 1:
                bit = lax.rem(a // (1 << i), 2)
                out = out + (1 << i) * (1 - 2 * bit)
        return out

    peer = [flip(me, s, 3) for s in range(SHARE)]
    mate = [(flip(z, s >> 1, 3), flip(core, s & 1, 1)) for s in range(16)]

    def mate_rep(s):
        return mate[s][0] * 4 + xh * 2 + mate[s][1]

    across = z * 4 + (1 - xh) * 2 + core

    local = [
        pltpu.make_async_copy(depth, depthv, lsem.at[0]),
        pltpu.make_async_copy(trow, idxv.at[0], lsem.at[1]),
        pltpu.make_async_copy(tcol, idxv.at[1], lsem.at[2]),
        pltpu.make_async_copy(tfr, idxv.at[2], lsem.at[3]),
        pltpu.make_async_copy(tcam, idxv.at[3], lsem.at[4]),
        pltpu.make_async_copy(poses, posev, lsem.at[5]),
        pltpu.make_async_copy(gain.at[:, pl.ds(me * DS, DS)], gainv, lsem.at[6]),
        pltpu.make_async_copy(frag.at[0], fragv, lsem.at[7]),
        pltpu.make_async_copy(glob, globv, lsem.at[8]),
        pltpu.make_async_copy(mom, momv, lsem.at[9]),
        pltpu.make_async_copy(
            weight.at[0, :, pl.ds(me * DS, DS)], wv.at[pl.ds(me * ROWS, ROWS)], lsem.at[10]
        ),
    ]
    for copy in local:
        copy.start()

    barrier = pltpu.get_barrier_semaphore()
    for s in range(1, SHARE):
        pl.semaphore_signal(barrier, inc=1, device_id=(rep, peer[s]), device_id_type=MESH)
    for s in range(1, 16):
        pl.semaphore_signal(barrier, inc=1, device_id=(mate_rep(s), me), device_id_type=MESH)
    pl.semaphore_signal(barrier, inc=1, device_id=(across, me), device_id_type=MESH)
    pl.semaphore_wait(barrier, SHARE - 1 + 15 + 1)

    def remote(src, dst, send, recv, device):
        return pltpu.make_async_remote_copy(
            src_ref=src, dst_ref=dst, send_sem=send, recv_sem=recv, device_id=device, device_id_type=MESH
        )

    w_copies = [
        remote(
            weight.at[0, :, pl.ds(peer[s] * DS, DS)],
            wv.at[pl.ds(me * ROWS, ROWS)],
            w_s.at[s], w_r.at[s], (rep, peer[s]),
        )
        for s in range(1, SHARE)
    ]
    for copy in w_copies:
        copy.start()

    for i in range(5):
        local[i].wait()
    msg[me, pl.ds(0, TOK), :] = depthv[...].T.astype(BF16)
    spot = jnp.concatenate(
        [
            (idxv[3] * NFRAME + idxv[2]).astype(F32),
            idxv[1].astype(F32),
            idxv[0].astype(F32),
            jnp.zeros((10, 128), F32),
        ],
        axis=0,
    )
    msg[me, pl.ds(TOK, 16), :] = spot.astype(BF16)
    msg_copies = [
        remote(msg.at[me], msg.at[me], msg_s.at[s], msg_r.at[s], (rep, peer[s]))
        for s in range(1, SHARE)
    ]
    for copy in msg_copies:
        copy.start()

    def main_copies(c):
        out = []
        for k, (src, dst) in enumerate(((tok, tokv), (cot, cotv))):
            for s in range(SHARE):
                source = src.at[pl.ds(c * TC, TC), pl.ds(peer[s] * DS, DS)]
                target = dst.at[c, pl.ds(pl.multiple_of(me * TC, TC), TC)]
                if s == 0:
                    out.append(pltpu.make_async_copy(source, target, main_r.at[c, k, 0]))
                else:
                    out.append(
                        remote(source, target, main_s.at[c, k, s], main_r.at[c, k, s], (rep, peer[s]))
                    )
        return out

    mains = [main_copies(c) for c in range(CHUNKS)]
    for c in range(2):
        for copy in mains[c]:
            copy.start()

    local[7].wait()
    chosen[...] = fragv[block[0]]
    f_copies = [
        remote(
            chosen.at[pl.ds(mate[s][0] * FP, FP), pl.ds(mate[s][1] * 128, 128)],
            fpart.at[s],
            f_s.at[s], f_r.at[s], (mate_rep(s), me),
        )
        for s in range(1, 16)
    ]
    for copy in f_copies:
        copy.start()

    local[5].wait()
    pixel = lax.broadcasted_iota(jnp.int32, (1, PIX), 1)
    sub_rows = PIX // 16
    horiz = (lax.rem(pixel, 16).astype(F32) + 0.5) / (GW * 16) * 2.0 - 1.0
    vert = ((pixel // 16).astype(F32) + 0.5) / (GH * sub_rows) * 2.0 - 1.0
    table_hi[...] = jnp.zeros_like(table_hi)
    table_lo[...] = jnp.zeros_like(table_lo)

    def put(part, channel, value):
        high = value.astype(BF16)
        where = (pl.ds(part * 128, POSES), pl.ds(channel * PIX, PIX))
        table_hi[where] = high
        table_lo[where] = (value - high.astype(F32)).astype(BF16)

    def entry(k):
        return jnp.broadcast_to(posev[k], (128, POSES)).T

    for ch in range(3):
        first, second, third = entry(3 * ch), entry(3 * ch + 1), entry(3 * ch + 2)
        put(0, ch, first * horiz + second * vert + third)
        put(1, ch, first * (2.0 / GW))
        put(2, ch, second * (2.0 / GH))
        put(0, 3 + ch, entry(9 + ch))

    for copy in msg_copies:
        copy.wait_recv()

    lane = lax.broadcasted_iota(jnp.int32, (128, 128), 1).astype(F32)

    def ray_block(s, _):
        spots = msg[s, pl.ds(TOK, 16), :].astype(F32)
        for half in range(2):
            hot = jnp.where(spread(spots[half : half + 1]) == lane, 1.0, 0.0)
            left = jnp.concatenate(
                [
                    hot,
                    hot * spread(spots[2 + half : 3 + half]),
                    hot * spread(spots[4 + half : 5 + half]),
                ],
                axis=1,
            ).astype(BF16)
            geo = jnp.dot(left, table_hi[...], preferred_element_type=F32) + jnp.dot(
                left, table_lo[...], preferred_element_type=F32
            )
            d = [geo[:, i * PIX : (i + 1) * PIX] for i in range(6)]
            far = msg[s, pl.ds(half * 128, 128), :].astype(F32)
            inv = lax.rsqrt(d[0] * d[0] + d[1] * d[1] + d[2] * d[2])
            near = inv / far
            long = inv * far
            for i in range(6):
                value = (d[i] * near if i < 3 else d[i] + d[i - 3] * long).astype(BF16)
                for q in range(128 // TC):
                    c = half * (128 // TC) + q
                    start = pl.multiple_of(s * TC, TC)
                    rays_t[c, pl.ds(start, TC), pl.ds(i * PIX, PIX)] = value[q * TC : (q + 1) * TC]
        return 0

    lax.fori_loop(0, SHARE, ray_block, 0)

    def turn(k, _):
        c, b = k // (CT // 128), lax.rem(k, CT // 128)
        start = pl.multiple_of(b * 128, 128)
        rays[c, :, pl.ds(start, 128)] = rays_t[c, pl.ds(start, 128), :].T
        return 0

    lax.fori_loop(0, CHUNKS * (CT // 128), turn, 0)

    for copy in f_copies:
        copy.wait_recv()
    total = chosen[pl.ds(pl.multiple_of(z * FP, 16), FP), pl.ds(pl.multiple_of(core * 128, 128), 128)].astype(F32)
    for s in range(1, 16):
        total = total + fpart[s].astype(F32)
    fsum[...] = total
    h_copy = remote(fsum, fother, h_s.at[0], h_r.at[0], (across, me))
    h_copy.start()

    for copy in w_copies:
        copy.wait_recv()
    local[6].wait()
    local[10].wait()
    gain_row = gainv[...]
    gacc[...] = jnp.zeros_like(gacc)

    b_copies = []

    def forward(c):
        def body(b, _):
            at = pl.ds(pl.multiple_of(b * 128, 128), 128)
            lifted = jnp.dot(rays_t[c, at, :], wv[...], preferred_element_type=F32)
            hidden = tokv[c, at, :].astype(F32) + lifted
            hid[c, at, :] = hidden
            square = hidden * hidden
            cross = hidden * (cotv[c, at, :].astype(F32) * gain_row)
            q1, q2 = square[:, :128], cross[:, :128]
            for k in range(1, DS // 128):
                q1 = q1 + square[:, k * 128 : (k + 1) * 128]
                q2 = q2 + cross[:, k * 128 : (k + 1) * 128]
            stat[c, 0, pl.ds(b, 1), :] = jnp.sum(q1.T, axis=0, keepdims=True)
            stat[c, 0, pl.ds(b + CT // 128, 1), :] = jnp.sum(q2.T, axis=0, keepdims=True)
            return 0

        lax.fori_loop(0, CT // 128, body, 0)

    def stat_copies(c):
        return [
            remote(stat.at[c, 0], stat.at[c, s], st_s.at[c, s], st_r.at[c, s], (rep, peer[s]))
            for s in range(1, SHARE)
        ]

    def backward(c):
        both = stat[c, 0]
        for s in range(1, SHARE):
            both = both + stat[c, s]
        scale = lax.rsqrt(both[: CT // 128] / D + EPS)
        pull = scale * scale * scale * (both[CT // 128 :] / D)
        for b in range(CT // 128):
            wide = spread(scale[b : b + 1])
            wide_pull = spread(pull[b : b + 1])
            at = pl.ds(b * 128, 128)
            for k in range(DS // 128):
                cols = pl.ds(k * 128, 128)
                hidden = hid[c, at, cols]
                up = cotv[c, at, cols].astype(F32) * wide
                slope[at, cols] = (up * gainv[:, cols] - wide_pull * hidden).astype(BF16)
                prod = up * hidden
                part = prod[0:8]
                for i in range(1, 16):
                    part = part + prod[i * 8 : (i + 1) * 8]
                gacc[:, cols] += part

    def spend(c):
        def body(i, _):
            at = pl.ds(pl.multiple_of(i * 192, 192), 192)
            new = jnp.dot(rays[c, at, :], slope[...], preferred_element_type=F32)
            if c == 0:
                acc[at, :] = new
            else:
                acc[at, :] += new
            return 0

        lax.fori_loop(0, PIN // 192, body, 0)

    stats = [stat_copies(c) for c in range(CHUNKS)]
    for c in range(CHUNKS):
        for copy in mains[c]:
            copy.wait_recv() if copy.is_remote else copy.wait()
        if c + 2 < CHUNKS:
            for copy in mains[c]:
                if copy.is_remote:
                    copy.wait_send()
            for copy in mains[c + 2]:
                copy.start()
        forward(c)
        for copy in stats[c]:
            copy.start()
        if c == 0:
            h_copy.wait_recv()
            avg[pl.ds(pl.multiple_of(z * FP, 16), FP), pl.ds(pl.multiple_of(core * 128, 128), 128)] = (
                (fsum[...] + fother[...]) * (1.0 / N_REP)
            ).astype(BF16)
            own = avg.at[pl.ds(z * FP, FP), pl.ds(core * 128, 128)]
            b_copies += [
                remote(own, own, b_s.at[s], b_r.at[s], (mate_rep(s), me)) for s in range(1, 16)
            ]
            for copy in b_copies:
                copy.start()
        if c == 2:
            for copy in b_copies:
                copy.wait_recv()
            local[8].wait()
            local[9].wait()

            def nesterov(i, _):
                at = pl.ds(pl.multiple_of(i * 64, 64), 64)
                delta = globv[at, :] - avg[at, :].astype(F32)
                moment = MOMENTUM_RATE * momv[at, :] + delta
                new = globv[at, :] - OUTER_RATE * (MOMENTUM_RATE * moment + delta)
                momv[at, :] = moment
                globv[at, :] = new
                mergedv[at, :] = (
                    MIX_RATE * chosen[at, :].astype(F32) + (1.0 - MIX_RATE) * new
                ).astype(BF16)
                return 0

            lax.fori_loop(0, FR // 64, nesterov, 0)
            outs = [
                pltpu.make_async_copy(globv, glob_out, lsem.at[8]),
                pltpu.make_async_copy(momv, mom_out, lsem.at[9]),
                pltpu.make_async_copy(mergedv, merged_out.at[0], lsem.at[7]),
            ]
            for copy in outs:
                copy.start()
        if c > 0:
            for copy in stats[c - 1]:
                copy.wait_recv()
            backward(c - 1)
            spend(c - 1)
    last = CHUNKS - 1
    for copy in stats[last]:
        copy.wait_recv()
    backward(last)

    g_copies = []
    for k in (1, 2, 3, 0):
        pair = flip(me // 2, k, 2)
        at = pl.ds(pl.multiple_of(pair * 192, 192), 192)
        grad[at, :] = (
            acc[at, :] + jnp.dot(rays[last, at, :], slope[...], preferred_element_type=F32)
        ).astype(BF16)
        for s in (2 * k, 2 * k + 1):
            source = grad.at[pl.ds(peer[s] * ROWS, ROWS)]
            target = grad_out.at[0, :, pl.ds(me * DS, DS)]
            if s == 0:
                mine = pltpu.make_async_copy(source, target, lsem.at[10])
                mine.start()
            else:
                copy = remote(source, target, g_s.at[s], g_r.at[s], (rep, peer[s]))
                copy.start()
                g_copies.append(copy)
    gainv[...] = jnp.sum(gacc[...], axis=0, keepdims=True)
    gain_copy = pltpu.make_async_copy(gainv, gain_out, lsem.at[6])
    gain_copy.start()

    for copy in outs:
        copy.wait()
    gain_copy.wait()
    mine.wait()
    for copy in w_copies + msg_copies + f_copies + [h_copy] + b_copies:
        copy.wait_send()
    for c in range(CHUNKS):
        if c + 2 >= CHUNKS:
            for copy in mains[c]:
                if copy.is_remote:
                    copy.wait_send()
        for copy in stats[c]:
            copy.wait_send()
    for copy in g_copies:
        copy.wait()


def shards(
    tokens, cotangent, token_row, token_col, token_frame, token_camera, pixel_depth,
    cam_poses, cam_weight, gain, frag_stack, frag_block, global_frag, momentum,
):
    dma = pltpu.SemaphoreType.DMA
    hbm = pl.BlockSpec(memory_space=pltpu.HBM)
    places = [a.reshape(2, 128) for a in (token_row, token_col, token_frame, token_camera)]
    return pl.pallas_call(
        kernel,
        name="step",
        out_shape=(
            jax.ShapeDtypeStruct((1, ROWS, D), BF16),
            jax.ShapeDtypeStruct((1, DS), F32),
            jax.ShapeDtypeStruct((FR, 256), F32),
            jax.ShapeDtypeStruct((FR, 256), F32),
            jax.ShapeDtypeStruct((1, FR, 256), BF16),
        ),
        in_specs=[hbm] * 11 + [pl.BlockSpec(memory_space=pltpu.SMEM)] + [hbm] * 2,
        out_specs=(hbm,) * 5,
        scratch_shapes=[
            pltpu.VMEM((CHUNKS, CT, DS), BF16),
            pltpu.VMEM((CHUNKS, CT, DS), BF16),
            pltpu.VMEM((PIN, DS), BF16),
            pltpu.VMEM((SHARE, MSG, 128), BF16),
            pltpu.VMEM((PIX, TOK), F32),
            pltpu.VMEM((4, 2, 128), jnp.int32),
            pltpu.VMEM((12, 1, POSES), F32),
            pltpu.VMEM((1, DS), F32),
            pltpu.VMEM((384, PIN), BF16),
            pltpu.VMEM((384, PIN), BF16),
            pltpu.VMEM((CHUNKS, CT, PIN), BF16),
            pltpu.VMEM((CHUNKS, PIN, CT), BF16),
            pltpu.VMEM((CHUNKS, CT, DS), F32),
            pltpu.VMEM((CT, DS), BF16),
            pltpu.VMEM((PIN, DS), F32),
            pltpu.VMEM((PIN, DS), BF16),
            pltpu.VMEM((8, DS), F32),
            pltpu.VMEM((CHUNKS, SHARE, 2 * CT // 128, 128), F32),
            pltpu.VMEM((6, FR, 256), BF16),
            pltpu.VMEM((FR, 256), BF16),
            pltpu.VMEM((16, FP, 128), BF16),
            pltpu.VMEM((FP, 128), F32),
            pltpu.VMEM((FP, 128), F32),
            pltpu.VMEM((FR, 256), BF16),
            pltpu.VMEM((FR, 256), F32),
            pltpu.VMEM((FR, 256), F32),
            pltpu.VMEM((FR, 256), BF16),
            dma((11,)),
            dma((CHUNKS, 2, SHARE)), dma((CHUNKS, 2, SHARE)),
            dma((SHARE,)), dma((SHARE,)),
            dma((SHARE,)), dma((SHARE,)),
            dma((CHUNKS, SHARE)), dma((CHUNKS, SHARE)),
            dma((SHARE,)), dma((SHARE,)),
            dma((16,)), dma((16,)),
            dma((1,)), dma((1,)),
            dma((16,)), dma((16,)),
        ],
        compiler_params=pltpu.CompilerParams(
            collective_id=0, has_side_effects=True, vmem_limit_bytes=60 << 20
        ),
        cost_estimate=pl.CostEstimate(flops=6 << 30, bytes_accessed=20 << 20, transcendentals=0),
    )(
        tokens, cotangent, *places, pixel_depth, cam_poses.transpose(1, 0, 2), cam_weight, gain,
        frag_stack, frag_block, global_frag, momentum,
    )


def solution(mesh):
    placed = (
        P(("rep", "fsdp"), None),
        P(("rep", "fsdp"), None),
        P(("rep", "fsdp")),
        P(("rep", "fsdp")),
        P(("rep", "fsdp")),
        P(("rep", "fsdp")),
        P(None, ("rep", "fsdp")),
        P("rep", None, None),
        P("rep", "fsdp", None),
        P("rep", None),
        P("rep", None, "fsdp", None),
        P(),
        P("fsdp", None),
        P("fsdp", None),
    )
    return jax.shard_map(
        shards,
        mesh=mesh,
        in_specs=placed,
        out_specs=(
            P("rep", "fsdp", None),
            P("rep", "fsdp"),
            P("fsdp", None),
            P("fsdp", None),
            P("rep", "fsdp", None),
        ),
        check_vma=False,
    )
```

time: 471 us -> 124 us (0.26)
  waiting for transfers between devices: 384 us -> 0 us
  Pallas kernels: 0 us -> 115 us
  blocking collectives: 33.2 us -> 0 us
  between operations: 18.2 us -> 0.66 us
  matrix products: 16 us -> 0 us
  other arithmetic: 15.4 us -> 0 us
    psum x1 -> x0, waiting for transfers between devices: 302 us -> none  [shards(): lax.psum(chosen.astype(jnp.bfloat16), 'rep').astype(jnp.float32) / replicas]
    pallas_call x0 -> x1, Pallas kernels: none -> 115 us  [shards(): pl.pallas_call(kernel, name='step', out_shape=(jax.ShapeDtypeStruct((1, R...]
    all_gather x1 -> x0, waiting for transfers between devices: 81.5 us -> none  [shards(): lax.all_gather(cam_weight[0], 'fsdp', axis=0, tiled=True)]
    unnamed x1 -> x0, blocking collectives: 33.2 us -> none
    dot_general x3 -> x0, matrix products: 16 us -> none  [the longest x1 8.12 us: shards(): jnp.dot(block, slope, preferred_element_type=jnp.float32)]
    unnamed x12 -> x9, local copies, waits for them, and re-layouts: 1.32 us -> 7.07 us
    unnamed x5 -> x0, other arithmetic: 5.73 us -> none
    broadcast_in_dim x2 -> x0, other arithmetic: 5.03 us -> none  [the longest x1 2.6 us: shards(): weight_grad.astype(jnp.bfloat16)[None]]
  transfers between devices with their start and end apart: 3 -> 0, of which waited for: 2 -> 0; matrix products, arithmetic and copies ran while one was open for 7% -> 0% of each run, Pallas kernels for 0% -> 0%
where the time goes in v1:
time: 124 us; the launch traced here: 123 us
  Pallas kernels  115 us (93%)
  local copies, waits for them, and re-layouts  7.07 us (6%)
    pallas_call x1, Pallas kernels, shards(): pl.pallas_call(kernel, name='step', out_shape=(jax.ShapeDtypeStruct((1, R...  115 us
    unnamed x9, local copies, waits for them, and re-layouts  7.07 us

profile of v1, /device:TPU:2, one launch (start us, length us, event | category | flops | bytes accessed | tf_op | source)
XLA Modules:
  0.0 123.2 jit_solution(11062174803681333838)
XLA Ops:
  0.6 115.4 %step.1 = (bf16[1,96,5120]{2,1,0:T(8,128)(2,1)}, f32[1,640]{1,0:T(1,128)}, f32[640,256]{1,0:T(8,128)}, f32[640,256]{1,0:T(8,128)}, bf16[1,640,256]{2,1,0:T(8,128)(2,1)}) custom-call(bf16[256,5120]{1,0:T(8,128)(2,1)} %tok.1, bf16[256,5120]{1,0:T(8,128)(2,1)} %cot.1, s32[2,128]{1,0:T(2,128)} %bitcast.6, s32[2,128]{1,0:T(2,128)} %bitcast.7, s32[2,128]{1,0:T(2,128)} %bitcast.8, ...), custom_call_target="tpu_custom_call" | custom-call | flops 6442450944 | bytes 20971520 | tf_op jit(solution)/shard_map/step/pallas_call | solution.py:410
  116.1 0.0 copy-start
  116.1 0.0 copy-start.1
  116.1 2.3 %copy.24 = bf16[1,96,5120]{2,1,0:T(8,128)(2,1)} copy(bf16[1,96,5120]{2,1,0:T(8,128)(2,1)} %get-tuple-element.10) | data formatting | bytes 1966080
  118.4 1.2 %copy.25 = f32[1,640]{1,0:T(1,128)} copy(f32[1,640]{1,0:T(1,128)} %get-tuple-element.11) | data formatting | bytes 5120
  119.7 2.0 %copy.26 = f32[640,256]{1,0:T(8,128)} copy(f32[640,256]{1,0:T(8,128)} %get-tuple-element.12) | data formatting | bytes 1310720
  121.6 0.0 copy-done
  121.6 0.8 copy.27
  122.5 0.0 copy-done.1
  122.5 0.7 copy.28
Async XLA Ops:
  116.1 5.5 %copy-start = (f32[640,256]{1,0:T(8,128)S(1)}, f32[640,256]{1,0:T(8,128)}, u32[]{:S(2)}) copy-start(f32[640,256]{1,0:T(8,128)} %get-tuple-element.13) | copy-start | bytes 1966084
  116.1 6.4 %copy-start.1 = (bf16[1,640,256]{2,1,0:T(8,128)(2,1)S(1)}, bf16[1,640,256]{2,1,0:T(8,128)(2,1)}, u32[]{:S(2)}) copy-start(bf16[1,640,256]{2,1,0:T(8,128)(2,1)} %get-tuple-element.14) | copy-start | bytes 983044

commit v2 on v1

--- a/solution.py
+++ b/solution.py
@@ -43,9 +43,9 @@
     grad_out, gain_out, glob_out, mom_out, merged_out,
     tokv, cotv, wv, msg, depthv, idxv, posev, gainv, table_hi, table_lo,
     rays_t, rays, hid, slope, acc, grad, gacc, stat,
-    fragv, chosen, fpart, fsum, fother, avg, globv, momv, mergedv,
+    fragv, chosen, fpart, fsum, fother, avg, globv, momv,
     lsem, main_s, main_r, w_s, w_r, msg_s, msg_r, st_s, st_r, g_s, g_r,
-    f_s, f_r, h_s, h_r, b_s, b_r,
+    f_s, f_r, h_s, h_r, b_s, b_r, ready, crossed,
 ):
     rep, me = lax.axis_index("rep"), lax.axis_index("fsdp")
     z, xh, core = rep // 4, lax.rem(rep // 2, 2), lax.rem(rep, 2)
@@ -86,11 +86,22 @@
 
     barrier = pltpu.get_barrier_semaphore()
     for s in range(1, SHARE):
-        pl.semaphore_signal(barrier, inc=1, device_id=(rep, peer[s]), device_id_type=MESH)
-    for s in range(1, 16):
-        pl.semaphore_signal(barrier, inc=1, device_id=(mate_rep(s), me), device_id_type=MESH)
-    pl.semaphore_signal(barrier, inc=1, device_id=(across, me), device_id_type=MESH)
-    pl.semaphore_wait(barrier, SHARE - 1 + 15 + 1)
+
+        @pl.when(peer[s] != 0)
+        def _():
+            pl.semaphore_signal(barrier, inc=1, device_id=(rep, peer[s]), device_id_type=MESH)
+
+    @pl.when(me != 0)
+    def _():
+        pl.semaphore_wait(barrier, SHARE - 1)
+        pl.semaphore_signal(ready, inc=1, device_id=(rep, 0), device_id_type=MESH)
+
+    @pl.when(me == 0)
+    def _():
+        pl.semaphore_wait(ready, SHARE - 1)
+        for s in range(1, 16):
+            pl.semaphore_signal(barrier, inc=1, device_id=(mate_rep(s), me), device_id_type=MESH)
+        pl.semaphore_signal(barrier, inc=1, device_id=(across, me), device_id_type=MESH)
 
     def remote(src, dst, send, recv, device):
         return pltpu.make_async_remote_copy(
@@ -157,8 +168,59 @@
         )
         for s in range(1, 16)
     ]
-    for copy in f_copies:
-        copy.start()
+    h_copy = remote(fsum, fother, h_s.at[0], h_r.at[0], (across, me))
+    piece = (pl.ds(pl.multiple_of(z * FP, 16), FP), pl.ds(pl.multiple_of(core * 128, 128), 128))
+    own = avg.at[piece]
+    b_copies = [remote(own, own, b_s.at[s], b_r.at[s], (mate_rep(s), me)) for s in range(1, 16)]
+
+    def scatter():
+        @pl.when(me == 0)
+        def _():
+            pl.semaphore_wait(barrier, 16)
+            for s in range(1, SHARE):
+                pl.semaphore_signal(crossed, inc=1, device_id=(rep, peer[s]), device_id_type=MESH)
+
+        @pl.when(me != 0)
+        def _():
+            pl.semaphore_wait(crossed, 1)
+
+        for copy in f_copies:
+            copy.start()
+
+    def exchange():
+        for copy in f_copies:
+            copy.wait_recv()
+        total = chosen[piece].astype(F32)
+        for s in range(1, 16):
+            total = total + fpart[s].astype(F32)
+        fsum[...] = total
+        h_copy.start()
+
+    def spread_average():
+        h_copy.wait_recv()
+        avg[piece] = ((fsum[...] + fother[...]) * (1.0 / N_REP)).astype(BF16)
+        for copy in b_copies:
+            copy.start()
+
+    def nesterov():
+        for copy in b_copies:
+            copy.wait_recv()
+        local[8].wait()
+        local[9].wait()
+
+        def body(i, _):
+            at = pl.ds(pl.multiple_of(i * 64, 64), 64)
+            delta = globv[at, :] - avg[at, :].astype(F32)
+            moment = MOMENTUM_RATE * momv[at, :] + delta
+            new = globv[at, :] - OUTER_RATE * (MOMENTUM_RATE * moment + delta)
+            mom_out[at, :] = moment
+            glob_out[at, :] = new
+            merged_out[0, at, :] = (
+                MIX_RATE * chosen[at, :].astype(F32) + (1.0 - MIX_RATE) * new
+            ).astype(BF16)
+            return 0
+
+        lax.fori_loop(0, FR // 64, body, 0)
 
     local[5].wait()
     pixel = lax.broadcasted_iota(jnp.int32, (1, PIX), 1)
@@ -227,23 +289,12 @@
 
     lax.fori_loop(0, CHUNKS * (CT // 128), turn, 0)
 
-    for copy in f_copies:
-        copy.wait_recv()
-    total = chosen[pl.ds(pl.multiple_of(z * FP, 16), FP), pl.ds(pl.multiple_of(core * 128, 128), 128)].astype(F32)
-    for s in range(1, 16):
-        total = total + fpart[s].astype(F32)
-    fsum[...] = total
-    h_copy = remote(fsum, fother, h_s.at[0], h_r.at[0], (across, me))
-    h_copy.start()
-
     for copy in w_copies:
         copy.wait_recv()
     local[6].wait()
     local[10].wait()
     gain_row = gainv[...]
     gacc[...] = jnp.zeros_like(gacc)
-
-    b_copies = []
 
     def forward(c):
         def body(b, _):
@@ -316,42 +367,11 @@
         for copy in stats[c]:
             copy.start()
         if c == 0:
-            h_copy.wait_recv()
-            avg[pl.ds(pl.multiple_of(z * FP, 16), FP), pl.ds(pl.multiple_of(core * 128, 128), 128)] = (
-                (fsum[...] + fother[...]) * (1.0 / N_REP)
-            ).astype(BF16)
-            own = avg.at[pl.ds(z * FP, FP), pl.ds(core * 128, 128)]
-            b_copies += [
-                remote(own, own, b_s.at[s], b_r.at[s], (mate_rep(s), me)) for s in range(1, 16)
-            ]
-            for copy in b_copies:
-                copy.start()
+            scatter()
+        if c == 1:
+            exchange()
         if c == 2:
-            for copy in b_copies:
-                copy.wait_recv()
-            local[8].wait()
-            local[9].wait()
-
-            def nesterov(i, _):
-                at = pl.ds(pl.multiple_of(i * 64, 64), 64)
-                delta = globv[at, :] - avg[at, :].astype(F32)
-                moment = MOMENTUM_RATE * momv[at, :] + delta
-                new = globv[at, :] - OUTER_RATE * (MOMENTUM_RATE * moment + delta)
-                momv[at, :] = moment
-                globv[at, :] = new
-                mergedv[at, :] = (
-                    MIX_RATE * chosen[at, :].astype(F32) + (1.0 - MIX_RATE) * new
-                ).astype(BF16)
-                return 0
-
-            lax.fori_loop(0, FR // 64, nesterov, 0)
-            outs = [
-                pltpu.make_async_copy(globv, glob_out, lsem.at[8]),
-                pltpu.make_async_copy(momv, mom_out, lsem.at[9]),
-                pltpu.make_async_copy(mergedv, merged_out.at[0], lsem.at[7]),
-            ]
-            for copy in outs:
-                copy.start()
+            spread_average()
         if c > 0:
             for copy in stats[c - 1]:
                 copy.wait_recv()
@@ -379,13 +399,8 @@
                 copy = remote(source, target, g_s.at[s], g_r.at[s], (rep, peer[s]))
                 copy.start()
                 g_copies.append(copy)
-    gainv[...] = jnp.sum(gacc[...], axis=0, keepdims=True)
-    gain_copy = pltpu.make_async_copy(gainv, gain_out, lsem.at[6])
-    gain_copy.start()
-
-    for copy in outs:
-        copy.wait()
-    gain_copy.wait()
+    gain_out[...] = jnp.sum(gacc[...], axis=0, keepdims=True)
+    nesterov()
     mine.wait()
     for copy in w_copies + msg_copies + f_copies + [h_copy] + b_copies:
         copy.wait_send()
@@ -400,6 +415,15 @@
         copy.wait()
 
 
+def finish(*refs):
+    ins, outs, sem = refs[:5], refs[5:10], refs[10]
+    copies = [pltpu.make_async_copy(a, b, sem.at[i]) for i, (a, b) in enumerate(zip(ins, outs))]
+    for copy in copies:
+        copy.start()
+    for copy in copies:
+        copy.wait()
+
+
 def shards(
     tokens, cotangent, token_row, token_col, token_frame, token_camera, pixel_depth,
     cam_poses, cam_weight, gain, frag_stack, frag_block, global_frag, momentum,
@@ -407,18 +431,13 @@
     dma = pltpu.SemaphoreType.DMA
     hbm = pl.BlockSpec(memory_space=pltpu.HBM)
     places = [a.reshape(2, 128) for a in (token_row, token_col, token_frame, token_camera)]
-    return pl.pallas_call(
+    shapes = (((1, ROWS, D), BF16), ((1, DS), F32), ((FR, 256), F32), ((FR, 256), F32), ((1, FR, 256), BF16))
+    results = pl.pallas_call(
         kernel,
         name="step",
-        out_shape=(
-            jax.ShapeDtypeStruct((1, ROWS, D), BF16),
-            jax.ShapeDtypeStruct((1, DS), F32),
-            jax.ShapeDtypeStruct((FR, 256), F32),
-            jax.ShapeDtypeStruct((FR, 256), F32),
-            jax.ShapeDtypeStruct((1, FR, 256), BF16),
-        ),
+        out_shape=tuple(pltpu.VMEM(*one) for one in shapes),
         in_specs=[hbm] * 11 + [pl.BlockSpec(memory_space=pltpu.SMEM)] + [hbm] * 2,
-        out_specs=(hbm,) * 5,
+        out_specs=(pl.BlockSpec(memory_space=pltpu.VMEM),) * 5,
         scratch_shapes=[
             pltpu.VMEM((CHUNKS, CT, DS), BF16),
             pltpu.VMEM((CHUNKS, CT, DS), BF16),
@@ -446,7 +465,6 @@
             pltpu.VMEM((FR, 256), BF16),
             pltpu.VMEM((FR, 256), F32),
             pltpu.VMEM((FR, 256), F32),
-            pltpu.VMEM((FR, 256), BF16),
             dma((11,)),
             dma((CHUNKS, 2, SHARE)), dma((CHUNKS, 2, SHARE)),
             dma((SHARE,)), dma((SHARE,)),
@@ -456,15 +474,29 @@
             dma((16,)), dma((16,)),
             dma((1,)), dma((1,)),
             dma((16,)), dma((16,)),
+            pltpu.SemaphoreType.REGULAR, pltpu.SemaphoreType.REGULAR,
         ],
         compiler_params=pltpu.CompilerParams(
-            collective_id=0, has_side_effects=True, vmem_limit_bytes=60 << 20
+            collective_id=0, has_side_effects=True, vmem_limit_bytes=44 << 20
         ),
         cost_estimate=pl.CostEstimate(flops=6 << 30, bytes_accessed=20 << 20, transcendentals=0),
     )(
-        tokens, cotangent, *places, pixel_depth, cam_poses.transpose(1, 0, 2), cam_weight, gain,
-        frag_stack, frag_block, global_frag, momentum,
+        *[
+            pltpu.with_memory_space_constraint(a, pltpu.HBM)
+            for a in (
+                tokens, cotangent, *places, pixel_depth, cam_poses.transpose(1, 0, 2), cam_weight, gain, frag_stack
+            )
+        ],
+        *[pltpu.with_memory_space_constraint(a, pltpu.HBM) for a in (frag_block, global_frag, momentum)],
     )
+    return pl.pallas_call(
+        finish,
+        name="finish",
+        out_shape=tuple(jax.ShapeDtypeStruct(*one) for one in shapes),
+        in_specs=[pl.BlockSpec(memory_space=pltpu.VMEM)] * 5,
+        out_specs=(pl.BlockSpec(memory_space=pltpu.HBM),) * 5,
+        scratch_shapes=[dma((5,))],
+    )(*[pltpu.with_memory_space_constraint(a, pltpu.VMEM) for a in results])
 
 
 def solution(mesh):

time: 124 us -> 109 us (0.88)
  Pallas kernels: 115 us -> 107 us
  local copies, waits for them, and re-layouts: 7.07 us -> 0 us
    pallas_call x1 -> x2, Pallas kernels: 115 us -> 107 us  [the longest x1 106 us: shards(): pl.pallas_call(kernel, name='step', out_shape=tuple((pltpu.VMEM(*one) for...]
    unnamed x9 -> x0, local copies, waits for them, and re-layouts: 7.07 us -> none
where the time goes in v2:
time: 109 us; the launch traced here: 108 us
  Pallas kernels  107 us (98%)
    pallas_call x1, Pallas kernels, shards(): pl.pallas_call(kernel, name='step', out_shape=tuple((pltpu.VMEM(*one) for...  106 us

profile of v2, /device:TPU:2, one launch (start us, length us, event | category | flops | bytes accessed | tf_op | source)
XLA Modules:
  0.0 108.0 jit_solution(9385008461876545410)
XLA Ops:
  0.6 105.8 %step.1 = (bf16[1,96,5120]{2,1,0:T(8,128)(2,1)S(1)}, f32[1,640]{1,0:T(1,128)S(1)}, f32[640,256]{1,0:T(8,128)S(1)}, f32[640,256]{1,0:T(8,128)S(1)}, bf16[1,640,256]{2,1,0:T(8,128)(2,1)S(1)}) custom-call(bf16[256,5120]{1,0:T(8,128)(2,1)} %tok.1, bf16[256,5120]{1,0:T(8,128)(2,1)} %cot.1, s32[2,128]{1,0:T(2,128)} %bitcast.6, s32[2,128]{1,0:T(2,128)} %bitcast.7, ...), custom_call_target="tpu_custom_call" | custom-call | flops 6442450944 | bytes 20971520 | tf_op jit(solution)/shard_map/step/pallas_call | solution.py:435
  106.5 1.5 %finish.1 = (bf16[1,96,5120]{2,1,0:T(8,128)(2,1)}, f32[1,640]{1,0:T(1,128)}, f32[640,256]{1,0:T(8,128)}, f32[640,256]{1,0:T(8,128)}, bf16[1,640,256]{2,1,0:T(8,128)(2,1)}) custom-call(bf16[1,96,5120]{2,1,0:T(8,128)(2,1)S(1)} %get-tuple-element.10.refs_0_, f32[1,640]{1,0:T(1,128)S(1)} %get-tuple-element.11.refs_1_, f32[640,256]{1,0:T(8,128)S(1)} %get-tuple-element.12.refs_2_, ...), custom_call_target="tpu_custom_call" | custom-call | tf_op jit(solution)/shard_map/finish/pallas_call | solution.py:492

commit v3 on v2

--- a/solution.py
+++ b/solution.py
@@ -17,12 +17,22 @@
 DS = D // SHARE
 ROWS = PIN // SHARE
 TOK = 256
-CHUNKS = 4
-TC = TOK // CHUNKS
-CT = SHARE * TC
 FR = 640
 FP = 80
 MSG = TOK + 16
+
+WIDTH = (512, 384, 384)
+BASE = (0, 2048, 3584)
+PAIR = ((0, 1, 2, 3), (0, 1, 4, 5), (0, 3, 4, 7))
+TWIN = (4, 3, 1)
+CLASSES = range(3)
+GROUP = 4
+GT = GROUP * TOK
+
+SIZES = (64, 64, 64, 32, 32)
+STARTS = tuple(sum(SIZES[:c]) for c in range(len(SIZES)))
+CHUNKS = len(SIZES)
+AHEAD = 2
 
 EPS = 1e-06
 MOMENTUM_RATE = 0.9
@@ -38,28 +48,64 @@
     return jnp.broadcast_to(row, (128, 128)).T
 
 
+def flip(a, b):
+    out = a
+    for i in range(3):
+        if b >> i & 1:
+            out = out + (1 << i) * (1 - 2 * lax.rem(a // (1 << i), 2))
+    return out
+
+
+def gain_tile(device, place):
+    x, y = device // 4, device % 4
+    slots = (y, x * 2 + ((y >> 1 ^ y) & 1), x * 2 + (y >> 1))
+    for k in CLASSES:
+        tiles = WIDTH[k] // 128
+        if place < tiles:
+            return BASE[k] // 128 + slots[k] * tiles + place
+        place -= tiles
+
+
 def kernel(
     tok, cot, trow, tcol, tfr, tcam, depth, poses, weight, gain, frag, block, glob, mom,
     grad_out, gain_out, glob_out, mom_out, merged_out,
-    tokv, cotv, wv, msg, depthv, idxv, posev, gainv, table_hi, table_lo,
-    rays_t, rays, hid, slope, acc, grad, gacc, stat,
+    tok_a, tok_b, tok_c, cot_a, cot_b, cot_c, w_a, w_b, w_c, rt_a, rt_b, rt_c, rays_a, rays_b, rays_c,
+    hid_a, hid_b, hid_c, slope_a, slope_b, slope_c, acc_a, acc_b, acc_c, send_a, send_b, send_c,
+    part_a, part_b, part_c, last_a, last_b, last_c, gacc_a, gacc_b, gacc_c, gain_a, gain_b, gain_c,
+    msg, depthv, idxv, posev, table_hi, table_lo, rays_all, stat, scales, pulls, gains, gsum,
     fragv, chosen, fpart, fsum, fother, avg, globv, momv,
-    lsem, main_s, main_r, w_s, w_r, msg_s, msg_r, st_s, st_r, g_s, g_r,
-    f_s, f_r, h_s, h_r, b_s, b_r, ready, crossed,
+    lsem, wl_s, gl_s, main_s, main_r, w_s, w_r, v_s, v_r, msg_s, msg_r, st_s, st_r, p_s, p_r, g_s, g_r,
+    gg_s, gg_r, f_s, f_r, h_s, h_r, b_s, b_r, ready, crossed,
 ):
+    tokv, cotv, wv = (tok_a, tok_b, tok_c), (cot_a, cot_b, cot_c), (w_a, w_b, w_c)
+    rays_t, rays, hid = (rt_a, rt_b, rt_c), (rays_a, rays_b, rays_c), (hid_a, hid_b, hid_c)
+    slope, acc, send = (slope_a, slope_b, slope_c), (acc_a, acc_b, acc_c), (send_a, send_b, send_c)
+    part, last_out, gacc = (part_a, part_b, part_c), (last_a, last_b, last_c), (gacc_a, gacc_b, gacc_c)
+    gainv = (gain_a, gain_b, gain_c)
+
     rep, me = lax.axis_index("rep"), lax.axis_index("fsdp")
     z, xh, core = rep // 4, lax.rem(rep // 2, 2), lax.rem(rep, 2)
-
-    def flip(a, b, bits):
-        out = a
-        for i in range(bits):
-            if b >> i & 1:
-                bit = lax.rem(a // (1 << i), 2)
-                out = out + (1 << i) * (1 - 2 * bit)
-        return out
-
-    peer = [flip(me, s, 3) for s in range(SHARE)]
-    mate = [(flip(z, s >> 1, 3), flip(core, s & 1, 1)) for s in range(16)]
+    x, y = me // 4, lax.rem(me, 4)
+    high, low = y // 2, lax.rem(y, 2)
+    odd = high + low - 2 * high * low
+    peer = [flip(me, s) for s in range(SHARE)]
+    place = (y, x * 2 + odd, x * 2 + high)
+
+    def member(k, i):
+        if k == 0:
+            return x * 4 + i
+        s = i & 1
+        if k == 1:
+            return (i >> 1) * 4 + 2 * high + (1 - high if s else high)
+        return (i >> 1) * 4 + 2 * s + (1 - odd if s else odd)
+
+    def columns(k, at):
+        return pl.ds(pl.multiple_of(BASE[k] + at * WIDTH[k], 128), WIDTH[k])
+
+    def rows_of(device):
+        return pl.ds(pl.multiple_of(device * ROWS, 32), ROWS)
+
+    mate = [(flip(z, s >> 1), flip(core, s & 1)) for s in range(16)]
 
     def mate_rep(s):
         return mate[s][0] * 4 + xh * 2 + mate[s][1]
@@ -73,15 +119,20 @@
         pltpu.make_async_copy(tfr, idxv.at[2], lsem.at[3]),
         pltpu.make_async_copy(tcam, idxv.at[3], lsem.at[4]),
         pltpu.make_async_copy(poses, posev, lsem.at[5]),
-        pltpu.make_async_copy(gain.at[:, pl.ds(me * DS, DS)], gainv, lsem.at[6]),
-        pltpu.make_async_copy(frag.at[0], fragv, lsem.at[7]),
-        pltpu.make_async_copy(glob, globv, lsem.at[8]),
-        pltpu.make_async_copy(mom, momv, lsem.at[9]),
-        pltpu.make_async_copy(
-            weight.at[0, :, pl.ds(me * DS, DS)], wv.at[pl.ds(me * ROWS, ROWS)], lsem.at[10]
-        ),
+        pltpu.make_async_copy(frag.at[0], fragv, lsem.at[6]),
+        pltpu.make_async_copy(glob, globv, lsem.at[7]),
+        pltpu.make_async_copy(mom, momv, lsem.at[8]),
     ]
     for copy in local:
+        copy.start()
+    w_local = [
+        pltpu.make_async_copy(weight.at[0, :, columns(k, place[k])], wv[k].at[rows_of(me)], wl_s.at[k])
+        for k in CLASSES
+    ]
+    gain_local = [
+        pltpu.make_async_copy(gain.at[:, columns(k, place[k])], gainv[k], gl_s.at[k]) for k in CLASSES
+    ]
+    for copy in w_local + gain_local:
         copy.start()
 
     barrier = pltpu.get_barrier_semaphore()
@@ -109,15 +160,32 @@
         )
 
     w_copies = [
-        remote(
-            weight.at[0, :, pl.ds(peer[s] * DS, DS)],
-            wv.at[pl.ds(me * ROWS, ROWS)],
-            w_s.at[s], w_r.at[s], (rep, peer[s]),
-        )
-        for s in range(1, SHARE)
-    ]
-    for copy in w_copies:
-        copy.start()
+        [
+            remote(
+                weight.at[0, :, columns(k, flip(place[k], e))],
+                wv[k].at[rows_of(me)],
+                w_s.at[k, e], w_r.at[k, e], (rep, peer[PAIR[k][e]]),
+            )
+            for e in range(1, GROUP)
+        ]
+        for k in CLASSES
+    ]
+    for e in range(GROUP - 1):
+        for k in CLASSES:
+            w_copies[k][e].start()
+    v_copies = [
+        [
+            remote(
+                weight.at[0, :, columns(k, place[k])] if e == 0 else wv[k].at[rows_of(peer[PAIR[k][e]])],
+                wv[k].at[rows_of(peer[PAIR[k][e]])],
+                v_s.at[k, e], v_r.at[k, e], (rep, peer[TWIN[k]]),
+            )
+            for e in range(GROUP)
+        ]
+        for k in CLASSES
+    ]
+    for k in CLASSES:
+        v_copies[k][0].start()
 
     for i in range(5):
         local[i].wait()
@@ -132,33 +200,41 @@
         axis=0,
     )
     msg[me, pl.ds(TOK, 16), :] = spot.astype(BF16)
+    near = [s for s in range(1, SHARE) if s != 6]
     msg_copies = [
-        remote(msg.at[me], msg.at[me], msg_s.at[s], msg_r.at[s], (rep, peer[s]))
-        for s in range(1, SHARE)
+        remote(msg.at[me], msg.at[me], msg_s.at[s], msg_r.at[s], (rep, peer[s])) for s in near
     ]
     for copy in msg_copies:
         copy.start()
 
     def main_copies(c):
-        out = []
-        for k, (src, dst) in enumerate(((tok, tokv), (cot, cotv))):
-            for s in range(SHARE):
-                source = src.at[pl.ds(c * TC, TC), pl.ds(peer[s] * DS, DS)]
-                target = dst.at[c, pl.ds(pl.multiple_of(me * TC, TC), TC)]
-                if s == 0:
-                    out.append(pltpu.make_async_copy(source, target, main_r.at[c, k, 0]))
-                else:
-                    out.append(
-                        remote(source, target, main_s.at[c, k, s], main_r.at[c, k, s], (rep, peer[s]))
-                    )
-        return out
+        near_ones, far_ones = [], []
+        for n, (src, dsts) in enumerate(((tok, tokv), (cot, cotv))):
+            for e in (1, 2, 3, 0):
+                for k in CLASSES:
+                    source = src.at[pl.ds(STARTS[c], SIZES[c]), columns(k, flip(place[k], e))]
+                    start = pl.multiple_of(GROUP * STARTS[c] + place[k] * SIZES[c], 32)
+                    target = dsts[k].at[pl.ds(start, SIZES[c])]
+                    if e == 0:
+                        near_ones.append(pltpu.make_async_copy(source, target, main_r.at[c, n, k, 0]))
+                    else:
+                        far_ones.append(
+                            remote(
+                                source, target, main_s.at[c, n, k, e], main_r.at[c, n, k, e],
+                                (rep, peer[PAIR[k][e]]),
+                            )
+                        )
+        return near_ones, far_ones
 
     mains = [main_copies(c) for c in range(CHUNKS)]
-    for c in range(2):
-        for copy in mains[c]:
+
+    def start_main(c):
+        for copy in mains[c][1] + mains[c][0]:
             copy.start()
 
-    local[7].wait()
+    start_main(0)
+
+    local[6].wait()
     chosen[...] = fragv[block[0]]
     f_copies = [
         remote(
@@ -205,8 +281,8 @@
     def nesterov():
         for copy in b_copies:
             copy.wait_recv()
+        local[7].wait()
         local[8].wait()
-        local[9].wait()
 
         def body(i, _):
             at = pl.ds(pl.multiple_of(i * 64, 64), 64)
@@ -245,6 +321,13 @@
         put(1, ch, first * (2.0 / GW))
         put(2, ch, second * (2.0 / GH))
         put(0, 3 + ch, entry(9 + ch))
+
+    for e in range(1, GROUP):
+        for k in CLASSES:
+            w_copies[k][e - 1].wait_recv()
+            v_copies[k][e].start()
+    for c in range(1, AHEAD):
+        start_main(c)
 
     for copy in msg_copies:
         copy.wait_recv()
@@ -269,50 +352,64 @@
             d = [geo[:, i * PIX : (i + 1) * PIX] for i in range(6)]
             far = msg[s, pl.ds(half * 128, 128), :].astype(F32)
             inv = lax.rsqrt(d[0] * d[0] + d[1] * d[1] + d[2] * d[2])
-            near = inv / far
+            close = inv / far
             long = inv * far
             for i in range(6):
-                value = (d[i] * near if i < 3 else d[i] + d[i - 3] * long).astype(BF16)
-                for q in range(128 // TC):
-                    c = half * (128 // TC) + q
-                    start = pl.multiple_of(s * TC, TC)
-                    rays_t[c, pl.ds(start, TC), pl.ds(i * PIX, PIX)] = value[q * TC : (q + 1) * TC]
+                value = d[i] * close if i < 3 else d[i] + d[i - 3] * long
+                rays_all[s, pl.ds(half * 128, 128), pl.ds(i * PIX, PIX)] = value.astype(BF16)
         return 0
 
-    lax.fori_loop(0, SHARE, ray_block, 0)
-
-    def turn(k, _):
-        c, b = k // (CT // 128), lax.rem(k, CT // 128)
-        start = pl.multiple_of(b * 128, 128)
-        rays[c, :, pl.ds(start, 128)] = rays_t[c, pl.ds(start, 128), :].T
-        return 0
-
-    lax.fori_loop(0, CHUNKS * (CT // 128), turn, 0)
-
-    for copy in w_copies:
-        copy.wait_recv()
-    local[6].wait()
-    local[10].wait()
-    gain_row = gainv[...]
-    gacc[...] = jnp.zeros_like(gacc)
+    def ray_step(n, _):
+        return ray_block(lax.rem(me + n, SHARE), 0)
+
+    msg[peer[6]] = msg[me]
+    lax.fori_loop(0, SHARE, ray_step, 0)
+
+    for k in CLASSES:
+        for i in range(GROUP):
+            for c in range(CHUNKS):
+                at = GROUP * STARTS[c] + i * SIZES[c]
+                rays_t[k][pl.ds(at, SIZES[c]), :] = rays_all[member(k, i), pl.ds(STARTS[c], SIZES[c]), :]
+
+        def turn(b, _, k=k):
+            at = pl.ds(pl.multiple_of(b * 128, 128), 128)
+            rays[k][:, at] = rays_t[k][at, :].T
+            return 0
+
+        lax.fori_loop(0, GT // 128, turn, 0)
+
+    for k in CLASSES:
+        w_local[k].wait()
+        gain_local[k].wait()
+        gacc[k][...] = jnp.zeros_like(gacc[k])
+        for copy in v_copies[k]:
+            copy.wait_recv()
+
+    wide_lane = lax.broadcasted_iota(jnp.int32, (1, 128), 1)
 
     def forward(c):
-        def body(b, _):
-            at = pl.ds(pl.multiple_of(b * 128, 128), 128)
-            lifted = jnp.dot(rays_t[c, at, :], wv[...], preferred_element_type=F32)
-            hidden = tokv[c, at, :].astype(F32) + lifted
-            hid[c, at, :] = hidden
-            square = hidden * hidden
-            cross = hidden * (cotv[c, at, :].astype(F32) * gain_row)
-            q1, q2 = square[:, :128], cross[:, :128]
-            for k in range(1, DS // 128):
-                q1 = q1 + square[:, k * 128 : (k + 1) * 128]
-                q2 = q2 + cross[:, k * 128 : (k + 1) * 128]
-            stat[c, 0, pl.ds(b, 1), :] = jnp.sum(q1.T, axis=0, keepdims=True)
-            stat[c, 0, pl.ds(b + CT // 128, 1), :] = jnp.sum(q2.T, axis=0, keepdims=True)
-            return 0
-
-        lax.fori_loop(0, CT // 128, body, 0)
+        size = SIZES[c]
+        count = 128 // size
+        stat[c, 0] = jnp.zeros((SHARE, 128), F32)
+        for k in CLASSES:
+            for b in range(GROUP * size // 128):
+                at = pl.ds(GROUP * STARTS[c] + b * 128, 128)
+                lifted = jnp.dot(rays_t[k][at, :], wv[k][...], preferred_element_type=F32)
+                hidden = tokv[k][at, :].astype(F32) + lifted
+                hid[k][at, :] = hidden
+                square = hidden * hidden
+                cross = hidden * (cotv[k][at, :].astype(F32) * gainv[k][...])
+                q1, q2 = square[:, :128], cross[:, :128]
+                for t in range(1, WIDTH[k] // 128):
+                    q1 = q1 + square[:, t * 128 : (t + 1) * 128]
+                    q2 = q2 + cross[:, t * 128 : (t + 1) * 128]
+                r1 = jnp.sum(q1.T, axis=0, keepdims=True)
+                r2 = jnp.sum(q2.T, axis=0, keepdims=True)
+                for j in range(count):
+                    one = pltpu.roll(r1, (128 - j * size) % 128, 1)
+                    two = pltpu.roll(r2, (192 - j * size) % 128, 1)
+                    source = pl.ds(member(k, b * count + j), 1)
+                    stat[c, 0, source, :] += jnp.where(wide_lane < 64, one, two)
 
     def stat_copies(c):
         return [
@@ -321,48 +418,71 @@
         ]
 
     def backward(c):
+        size = SIZES[c]
+        count = 128 // size
         both = stat[c, 0]
         for s in range(1, SHARE):
             both = both + stat[c, s]
-        scale = lax.rsqrt(both[: CT // 128] / D + EPS)
-        pull = scale * scale * scale * (both[CT // 128 :] / D)
-        for b in range(CT // 128):
-            wide = spread(scale[b : b + 1])
-            wide_pull = spread(pull[b : b + 1])
-            at = pl.ds(b * 128, 128)
-            for k in range(DS // 128):
-                cols = pl.ds(k * 128, 128)
-                hidden = hid[c, at, cols]
-                up = cotv[c, at, cols].astype(F32) * wide
-                slope[at, cols] = (up * gainv[:, cols] - wide_pull * hidden).astype(BF16)
-                prod = up * hidden
-                part = prod[0:8]
-                for i in range(1, 16):
-                    part = part + prod[i * 8 : (i + 1) * 8]
-                gacc[:, cols] += part
+        scale = lax.rsqrt(both / D + EPS)
+        scales[...] = scale
+        pulls[...] = scale * scale * scale * (pltpu.roll(both, 64, 1) / D)
+
+        def gather(ref, k, b):
+            row = ref[pl.ds(member(k, b * count), 1), :]
+            for j in range(1, count):
+                other = pltpu.roll(ref[pl.ds(member(k, b * count + j), 1), :], j * size, 1)
+                row = jnp.where(wide_lane < j * size, row, other)
+            return spread(row)
+
+        for k in CLASSES:
+            for b in range(GROUP * size // 128):
+                wide = gather(scales, k, b)
+                wide_pull = gather(pulls, k, b)
+                at = pl.ds(GROUP * STARTS[c] + b * 128, 128)
+                for t in range(WIDTH[k] // 128):
+                    cols = pl.ds(t * 128, 128)
+                    hidden = hid[k][at, cols]
+                    up = cotv[k][at, cols].astype(F32) * wide
+                    slope[k][pl.ds(b * 128, 128), cols] = (
+                        up * gainv[k][:, cols] - wide_pull * hidden
+                    ).astype(BF16)
+                    prod = up * hidden
+                    part_sum = prod[0:8]
+                    for i in range(1, 16):
+                        part_sum = part_sum + prod[i * 8 : (i + 1) * 8]
+                    gacc[k][:, cols] += part_sum
+
+    def product(c, k, at):
+        count = GROUP * SIZES[c]
+        return jnp.dot(
+            rays[k][at, pl.ds(GROUP * STARTS[c], count)],
+            slope[k][pl.ds(0, count), :],
+            preferred_element_type=F32,
+        )
 
     def spend(c):
-        def body(i, _):
-            at = pl.ds(pl.multiple_of(i * 192, 192), 192)
-            new = jnp.dot(rays[c, at, :], slope[...], preferred_element_type=F32)
-            if c == 0:
-                acc[at, :] = new
-            else:
-                acc[at, :] += new
-            return 0
-
-        lax.fori_loop(0, PIN // 192, body, 0)
+        for k in CLASSES:
+
+            def body(i, _, k=k):
+                at = pl.ds(pl.multiple_of(i * 192, 192), 192)
+                if c == 0:
+                    acc[k][at, :] = product(c, k, at)
+                else:
+                    acc[k][at, :] += product(c, k, at)
+                return 0
+
+            lax.fori_loop(0, PIN // 192, body, 0)
 
     stats = [stat_copies(c) for c in range(CHUNKS)]
     for c in range(CHUNKS):
-        for copy in mains[c]:
-            copy.wait_recv() if copy.is_remote else copy.wait()
-        if c + 2 < CHUNKS:
-            for copy in mains[c]:
-                if copy.is_remote:
-                    copy.wait_send()
-            for copy in mains[c + 2]:
-                copy.start()
+        for copy in mains[c][1]:
+            copy.wait_recv()
+        for copy in mains[c][0]:
+            copy.wait()
+        if c + AHEAD < CHUNKS:
+            for copy in mains[c][1]:
+                copy.wait_send()
+            start_main(c + AHEAD)
         forward(c)
         for copy in stats[c]:
             copy.start()
@@ -382,33 +502,62 @@
         copy.wait_recv()
     backward(last)
 
+    p_copies = []
+    for k in CLASSES:
+        for e in range(GROUP):
+            at = rows_of(peer[TWIN[k] ^ PAIR[k][e]])
+            send[k][e] = (acc[k][at, :] + product(last, k, at)).astype(BF16)
+            copy = remote(send[k].at[e], part[k].at[e], p_s.at[k, e], p_r.at[k, e], (rep, peer[TWIN[k]]))
+            copy.start()
+            p_copies.append(copy)
+    for k in CLASSES:
+        for t in range(WIDTH[k] // 128):
+            n = sum(WIDTH[:k]) // 128 + t
+            gains[me, pl.ds(n, 1), :] = jnp.sum(gacc[k][:, pl.ds(t * 128, 128)], axis=0, keepdims=True)
+    gain_copies = [
+        remote(gains.at[me], gains.at[me], gg_s.at[s], gg_r.at[s], (rep, peer[s])) for s in range(1, SHARE)
+    ]
+    for copy in gain_copies:
+        copy.start()
     g_copies = []
-    for k in (1, 2, 3, 0):
-        pair = flip(me // 2, k, 2)
-        at = pl.ds(pl.multiple_of(pair * 192, 192), 192)
-        grad[at, :] = (
-            acc[at, :] + jnp.dot(rays[last, at, :], slope[...], preferred_element_type=F32)
-        ).astype(BF16)
-        for s in (2 * k, 2 * k + 1):
-            source = grad.at[pl.ds(peer[s] * ROWS, ROWS)]
-            target = grad_out.at[0, :, pl.ds(me * DS, DS)]
-            if s == 0:
-                mine = pltpu.make_async_copy(source, target, lsem.at[10])
-                mine.start()
+    for e in (1, 2, 3, 0):
+        for k in CLASSES:
+            at = rows_of(peer[PAIR[k][e]])
+            value = acc[k][at, :] + product(last, k, at)
+            p_copies[k * GROUP + e].wait_recv()
+            value = (value + part[k][e].astype(F32)).astype(BF16)
+            if e == 0:
+                grad_out[0, :, columns(k, place[k])] = value
             else:
-                copy = remote(source, target, g_s.at[s], g_r.at[s], (rep, peer[s]))
+                last_out[k][e - 1] = value
+                copy = remote(
+                    last_out[k].at[e - 1], grad_out.at[0, :, columns(k, place[k])],
+                    g_s.at[k, e], g_r.at[k, e], (rep, peer[PAIR[k][e]]),
+                )
                 copy.start()
                 g_copies.append(copy)
-    gain_out[...] = jnp.sum(gacc[...], axis=0, keepdims=True)
     nesterov()
-    mine.wait()
-    for copy in w_copies + msg_copies + f_copies + [h_copy] + b_copies:
+    for copy in gain_copies:
+        copy.wait_recv()
+    seen = set()
+    for s in range(SHARE):
+        for n in range(10):
+            tile = pl.ds(gain_tile(s, n), 1)
+            value = gains[s, pl.ds(n, 1), :]
+            gsum[tile, :] = gsum[tile, :] + value if gain_tile(s, n) in seen else value
+            seen.add(gain_tile(s, n))
+    for t in range(DS // 128):
+        gain_out[:, pl.ds(t * 128, 128)] = gsum[pl.ds(me * (DS // 128) + t, 1), :]
+
+    for k in CLASSES:
+        for copy in w_copies[k] + v_copies[k]:
+            copy.wait_send()
+    for copy in msg_copies + p_copies + gain_copies + f_copies + [h_copy] + b_copies:
         copy.wait_send()
     for c in range(CHUNKS):
-        if c + 2 >= CHUNKS:
-            for copy in mains[c]:
-                if copy.is_remote:
-                    copy.wait_send()
+        if c + AHEAD >= CHUNKS:
+            for copy in mains[c][1]:
+                copy.wait_send()
         for copy in stats[c]:
             copy.wait_send()
     for copy in g_copies:
@@ -439,24 +588,31 @@
         in_specs=[hbm] * 11 + [pl.BlockSpec(memory_space=pltpu.SMEM)] + [hbm] * 2,
         out_specs=(pl.BlockSpec(memory_space=pltpu.VMEM),) * 5,
         scratch_shapes=[
-            pltpu.VMEM((CHUNKS, CT, DS), BF16),
-            pltpu.VMEM((CHUNKS, CT, DS), BF16),
-            pltpu.VMEM((PIN, DS), BF16),
+            *[pltpu.VMEM((GT, w), BF16) for w in WIDTH],
+            *[pltpu.VMEM((GT, w), BF16) for w in WIDTH],
+            *[pltpu.VMEM((PIN, w), BF16) for w in WIDTH],
+            *[pltpu.VMEM((GT, PIN), BF16) for w in WIDTH],
+            *[pltpu.VMEM((PIN, GT), BF16) for w in WIDTH],
+            *[pltpu.VMEM((GT, w), F32) for w in WIDTH],
+            *[pltpu.VMEM((GROUP * max(SIZES), w), BF16) for w in WIDTH],
+            *[pltpu.VMEM((PIN, w), F32) for w in WIDTH],
+            *[pltpu.VMEM((GROUP, ROWS, w), BF16) for w in WIDTH],
+            *[pltpu.VMEM((GROUP, ROWS, w), BF16) for w in WIDTH],
+            *[pltpu.VMEM((GROUP - 1, ROWS, w), BF16) for w in WIDTH],
+            *[pltpu.VMEM((8, w), F32) for w in WIDTH],
+            *[pltpu.VMEM((1, w), F32) for w in WIDTH],
             pltpu.VMEM((SHARE, MSG, 128), BF16),
             pltpu.VMEM((PIX, TOK), F32),
             pltpu.VMEM((4, 2, 128), jnp.int32),
             pltpu.VMEM((12, 1, POSES), F32),
-            pltpu.VMEM((1, DS), F32),
             pltpu.VMEM((384, PIN), BF16),
             pltpu.VMEM((384, PIN), BF16),
-            pltpu.VMEM((CHUNKS, CT, PIN), BF16),
-            pltpu.VMEM((CHUNKS, PIN, CT), BF16),
-            pltpu.VMEM((CHUNKS, CT, DS), F32),
-            pltpu.VMEM((CT, DS), BF16),
-            pltpu.VMEM((PIN, DS), F32),
-            pltpu.VMEM((PIN, DS), BF16),
-            pltpu.VMEM((8, DS), F32),
-            pltpu.VMEM((CHUNKS, SHARE, 2 * CT // 128, 128), F32),
+            pltpu.VMEM((SHARE, TOK, PIN), BF16),
+            pltpu.VMEM((CHUNKS, SHARE, SHARE, 128), F32),
+            pltpu.VMEM((SHARE, 128), F32),
+            pltpu.VMEM((SHARE, 128), F32),
+            pltpu.VMEM((SHARE, 16, 128), F32),
+            pltpu.VMEM((D // 128, 128), F32),
             pltpu.VMEM((6, FR, 256), BF16),
             pltpu.VMEM((FR, 256), BF16),
             pltpu.VMEM((16, FP, 128), BF16),
@@ -465,11 +621,14 @@
             pltpu.VMEM((FR, 256), BF16),
             pltpu.VMEM((FR, 256), F32),
             pltpu.VMEM((FR, 256), F32),
-            dma((11,)),
-            dma((CHUNKS, 2, SHARE)), dma((CHUNKS, 2, SHARE)),
-            dma((SHARE,)), dma((SHARE,)),
+            dma((9,)), dma((3,)), dma((3,)),
+            dma((CHUNKS, 2, 3, GROUP)), dma((CHUNKS, 2, 3, GROUP)),
+            dma((3, GROUP)), dma((3, GROUP)),
+            dma((3, GROUP)), dma((3, GROUP)),
             dma((SHARE,)), dma((SHARE,)),
             dma((CHUNKS, SHARE)), dma((CHUNKS, SHARE)),
+            dma((3, GROUP)), dma((3, GROUP)),
+            dma((3, GROUP)), dma((3, GROUP)),
             dma((SHARE,)), dma((SHARE,)),
             dma((16,)), dma((16,)),
             dma((1,)), dma((1,)),
@@ -477,7 +636,7 @@
             pltpu.SemaphoreType.REGULAR, pltpu.SemaphoreType.REGULAR,
         ],
         compiler_params=pltpu.CompilerParams(
-            collective_id=0, has_side_effects=True, vmem_limit_bytes=44 << 20
+            collective_id=0, has_side_effects=True, vmem_limit_bytes=56 << 20
         ),
         cost_estimate=pl.CostEstimate(flops=6 << 30, bytes_accessed=20 << 20, transcendentals=0),
     )(

time: 109 us -> 100 us (0.917)
  Pallas kernels: 107 us -> 98.4 us
    pallas_call x1, Pallas kernels: 106 us -> 96.9 us  [shards(): pl.pallas_call(kernel, name='step', out_shape=tuple((pltpu.VMEM(*one) for...]
where the time goes in v3:
time: 100 us; the launch traced here: 99.2 us
  Pallas kernels  98.4 us (98%)
    pallas_call x1, Pallas kernels, shards(): pl.pallas_call(kernel, name='step', out_shape=tuple((pltpu.VMEM(*one) for...  96.9 us

profile of v3, /device:TPU:2, one launch (start us, length us, event | category | flops | bytes accessed | tf_op | source)
XLA Modules:
  0.0 99.2 jit_solution(7710314917730281935)
XLA Ops:
  0.6 96.9 %step.1 = (bf16[1,96,5120]{2,1,0:T(8,128)(2,1)S(1)}, f32[1,640]{1,0:T(1,128)S(1)}, f32[640,256]{1,0:T(8,128)S(1)}, f32[640,256]{1,0:T(8,128)S(1)}, bf16[1,640,256]{2,1,0:T(8,128)(2,1)S(1)}) custom-call(bf16[256,5120]{1,0:T(8,128)(2,1)} %tok.1, bf16[256,5120]{1,0:T(8,128)(2,1)} %cot.1, s32[2,128]{1,0:T(2,128)} %bitcast.6, s32[2,128]{1,0:T(2,128)} %bitcast.7, ...), custom_call_target="tpu_custom_call" | custom-call | flops 6442450944 | bytes 20971520 | tf_op jit(solution)/shard_map/step/pallas_call | solution.py:584
  97.5 1.5 %finish.1 = (bf16[1,96,5120]{2,1,0:T(8,128)(2,1)}, f32[1,640]{1,0:T(1,128)}, f32[640,256]{1,0:T(8,128)}, f32[640,256]{1,0:T(8,128)}, bf16[1,640,256]{2,1,0:T(8,128)(2,1)}) custom-call(bf16[1,96,5120]{2,1,0:T(8,128)(2,1)S(1)} %get-tuple-element.10.refs_0_, f32[1,640]{1,0:T(1,128)S(1)} %get-tuple-element.11.refs_1_, f32[640,256]{1,0:T(8,128)S(1)} %get-tuple-element.12.refs_2_, ...), custom_call_target="tpu_custom_call" | custom-call | tf_op jit(solution)/shard_map/finish/pallas_call | solution.py:651

commit v4 on v3

--- a/solution.py
+++ b/solution.py
@@ -29,10 +29,10 @@
 GROUP = 4
 GT = GROUP * TOK
 
-SIZES = (64, 64, 64, 32, 32)
+SIZES = (64, 64, 64, 64)
 STARTS = tuple(sum(SIZES[:c]) for c in range(len(SIZES)))
 CHUNKS = len(SIZES)
-AHEAD = 2
+ORDER = (((0,), (), (1,), (2, 3), (), ()), ((0,), (1, 2), (3,), (), (), ()))
 
 EPS = 1e-06
 MOMENTUM_RATE = 0.9
@@ -232,7 +232,16 @@
         for copy in mains[c][1] + mains[c][0]:
             copy.start()
 
-    start_main(0)
+    def start_some(step):
+        for n in range(2):
+            if ORDER[n][step]:
+
+                @pl.when(core == n)
+                def _():
+                    for c in ORDER[n][step]:
+                        start_main(c)
+
+    start_some(0)
 
     local[6].wait()
     chosen[...] = fragv[block[0]]
@@ -326,8 +335,7 @@
         for k in CLASSES:
             w_copies[k][e - 1].wait_recv()
             v_copies[k][e].start()
-    for c in range(1, AHEAD):
-        start_main(c)
+    start_some(1)
 
     for copy in msg_copies:
         copy.wait_recv()
@@ -479,10 +487,9 @@
             copy.wait_recv()
         for copy in mains[c][0]:
             copy.wait()
-        if c + AHEAD < CHUNKS:
-            for copy in mains[c][1]:
-                copy.wait_send()
-            start_main(c + AHEAD)
+        for copy in mains[c][1]:
+            copy.wait_send()
+        start_some(c + 2)
         forward(c)
         for copy in stats[c]:
             copy.start()
@@ -502,14 +509,14 @@
         copy.wait_recv()
     backward(last)
 
-    p_copies = []
-    for k in CLASSES:
-        for e in range(GROUP):
+    p_copies = {}
+    for e in (1, 2, 3, 0):
+        for k in CLASSES:
             at = rows_of(peer[TWIN[k] ^ PAIR[k][e]])
             send[k][e] = (acc[k][at, :] + product(last, k, at)).astype(BF16)
             copy = remote(send[k].at[e], part[k].at[e], p_s.at[k, e], p_r.at[k, e], (rep, peer[TWIN[k]]))
             copy.start()
-            p_copies.append(copy)
+            p_copies[k, e] = copy
     for k in CLASSES:
         for t in range(WIDTH[k] // 128):
             n = sum(WIDTH[:k]) // 128 + t
@@ -524,7 +531,7 @@
         for k in CLASSES:
             at = rows_of(peer[PAIR[k][e]])
             value = acc[k][at, :] + product(last, k, at)
-            p_copies[k * GROUP + e].wait_recv()
+            p_copies[k, e].wait_recv()
             value = (value + part[k][e].astype(F32)).astype(BF16)
             if e == 0:
                 grad_out[0, :, columns(k, place[k])] = value
@@ -552,12 +559,9 @@
     for k in CLASSES:
         for copy in w_copies[k] + v_copies[k]:
             copy.wait_send()
-    for copy in msg_copies + p_copies + gain_copies + f_copies + [h_copy] + b_copies:
+    for copy in msg_copies + list(p_copies.values()) + gain_copies + f_copies + [h_copy] + b_copies:
         copy.wait_send()
     for c in range(CHUNKS):
-        if c + AHEAD >= CHUNKS:
-            for copy in mains[c][1]:
-                copy.wait_send()
         for copy in stats[c]:
             copy.wait_send()
     for copy in g_copies:

time: 100 us -> 95.3 us (0.953)
  Pallas kernels: 98.4 us -> 93.7 us
    pallas_call x1, Pallas kernels: 96.9 us -> 92.1 us  [shards(): pl.pallas_call(kernel, name='step', out_shape=tuple((pltpu.VMEM(*one) for...]
where the time goes in v4:
time: 95.3 us; the launch traced here: 94.5 us
  Pallas kernels  93.7 us (98%)
    pallas_call x1, Pallas kernels, shards(): pl.pallas_call(kernel, name='step', out_shape=tuple((pltpu.VMEM(*one) for...  92.1 us

profile of v4, /device:TPU:2, one launch (start us, length us, event | category | flops | bytes accessed | tf_op | source)
XLA Modules:
  0.0 94.5 jit_solution(4605532464117192431)
XLA Ops:
  0.6 92.1 %step.1 = (bf16[1,96,5120]{2,1,0:T(8,128)(2,1)S(1)}, f32[1,640]{1,0:T(1,128)S(1)}, f32[640,256]{1,0:T(8,128)S(1)}, f32[640,256]{1,0:T(8,128)S(1)}, bf16[1,640,256]{2,1,0:T(8,128)(2,1)S(1)}) custom-call(bf16[256,5120]{1,0:T(8,128)(2,1)} %tok.1, bf16[256,5120]{1,0:T(8,128)(2,1)} %cot.1, s32[2,128]{1,0:T(2,128)} %bitcast.6, s32[2,128]{1,0:T(2,128)} %bitcast.7, ...), custom_call_target="tpu_custom_call" | custom-call | flops 6442450944 | bytes 20971520 | tf_op jit(solution)/shard_map/step/pallas_call | solution.py:588
  92.8 1.5 %finish.1 = (bf16[1,96,5120]{2,1,0:T(8,128)(2,1)}, f32[1,640]{1,0:T(1,128)}, f32[640,256]{1,0:T(8,128)}, f32[640,256]{1,0:T(8,128)}, bf16[1,640,256]{2,1,0:T(8,128)(2,1)}) custom-call(bf16[1,96,5120]{2,1,0:T(8,128)(2,1)S(1)} %get-tuple-element.10.refs_0_, f32[1,640]{1,0:T(1,128)S(1)} %get-tuple-element.11.refs_1_, f32[640,256]{1,0:T(8,128)S(1)} %get-tuple-element.12.refs_2_, ...), custom_call_target="tpu_custom_call" | custom-call | tf_op jit(solution)/shard_map/finish/pallas_call | solution.py:655

commit v5 on v4

--- a/solution.py
+++ b/solution.py
@@ -112,6 +112,13 @@
 
     across = z * 4 + (1 - xh) * 2 + core
 
+    barrier = pltpu.get_barrier_semaphore()
+    for s in range(1, SHARE):
+
+        @pl.when(peer[s] != 0)
+        def _():
+            pl.semaphore_signal(barrier, inc=1, device_id=(rep, peer[s]), device_id_type=MESH)
+
     local = [
         pltpu.make_async_copy(depth, depthv, lsem.at[0]),
         pltpu.make_async_copy(trow, idxv.at[0], lsem.at[1]),
@@ -134,13 +141,6 @@
     ]
     for copy in w_local + gain_local:
         copy.start()
-
-    barrier = pltpu.get_barrier_semaphore()
-    for s in range(1, SHARE):
-
-        @pl.when(peer[s] != 0)
-        def _():
-            pl.semaphore_signal(barrier, inc=1, device_id=(rep, peer[s]), device_id_type=MESH)
 
     @pl.when(me != 0)
     def _():

time: 95.3 us -> 95.2 us (level)
  no operation moved by 1% of the time
where the time goes in v5:
time: 95.2 us; the launch traced here: 94.4 us
  Pallas kernels  93.6 us (98%)
    pallas_call x1, Pallas kernels, shards(): pl.pallas_call(kernel, name='step', out_shape=tuple((pltpu.VMEM(*one) for...  92.1 us

profile of v5, /device:TPU:2, one launch (start us, length us, event | category | flops | bytes accessed | tf_op | source)
XLA Modules:
  0.0 94.4 jit_solution(6959948853207046652)
XLA Ops:
  0.6 92.1 %step.1 = (bf16[1,96,5120]{2,1,0:T(8,128)(2,1)S(1)}, f32[1,640]{1,0:T(1,128)S(1)}, f32[640,256]{1,0:T(8,128)S(1)}, f32[640,256]{1,0:T(8,128)S(1)}, bf16[1,640,256]{2,1,0:T(8,128)(2,1)S(1)}) custom-call(bf16[256,5120]{1,0:T(8,128)(2,1)} %tok.1, bf16[256,5120]{1,0:T(8,128)(2,1)} %cot.1, s32[2,128]{1,0:T(2,128)} %bitcast.6, s32[2,128]{1,0:T(2,128)} %bitcast.7, ...), custom_call_target="tpu_custom_call" | custom-call | flops 6442450944 | bytes 20971520 | tf_op jit(solution)/shard_map/step/pallas_call | solution.py:588
  92.7 1.5 %finish.1 = (bf16[1,96,5120]{2,1,0:T(8,128)(2,1)}, f32[1,640]{1,0:T(1,128)}, f32[640,256]{1,0:T(8,128)}, f32[640,256]{1,0:T(8,128)}, bf16[1,640,256]{2,1,0:T(8,128)(2,1)}) custom-call(bf16[1,96,5120]{2,1,0:T(8,128)(2,1)S(1)} %get-tuple-element.10.refs_0_, f32[1,640]{1,0:T(1,128)S(1)} %get-tuple-element.11.refs_1_, f32[640,256]{1,0:T(8,128)S(1)} %get-tuple-element.12.refs_2_, ...), custom_call_target="tpu_custom_call" | custom-call | tf_op jit(solution)/shard_map/finish/pallas_call | solution.py:655
